TPU v7x, 256 devices: a whole 4x4x8 slice. The times are simulated.
256 devices in a mesh: row: 32 (over z_lo, x, y), col: 8 (over z_hi, core).
Axes of the slice: x: 4, y: 4, z: 8 (z_hi: 4, z_lo: 2; z = z_hi * 2 + z_lo), core: 2. Of those that a mesh axis runs over, the one named last changes fastest.
Arguments:
- grad_out: bfloat16 [64, 512, 2048], P(None, 'row', 'col'), may hold values from -6 to 6
- row_feat: bfloat16 [512, 64], P('row'), may hold values from -6 to 6
- col_feat: bfloat16 [2048, 64], P('col'), may hold values from -6 to 6
- conv_one: bfloat16 [3, 3, 64, 64], replicated, may hold values from -0.25 to 0.25
- bias_one: float32 [64], replicated, may hold values from -3 to 3
- conv_two: bfloat16 [3, 3, 64, 64], replicated, may hold values from -0.25 to 0.25
Outputs:
- row_grad: float32 [512, 64], P('row')
- col_grad: float32 [2048, 64], P('col')
- grad_conv_one: float32 [3, 3, 64, 64], replicated
- grad_bias: float32 [64], replicated
- grad_conv_two: float32 [3, 3, 64, 64], replicated
All inputs are finite; a program needn't handle non-finite values.
Results may differ from a plain program's by a relative error of at most 0.0065.
Values may be sent and summed in bfloat16 or wider, within the bound.
No kernel may reach another device: no remote copies, remote signals or barrier semaphores. Data moves between devices by JAX's collectives and lax.ppermute only.
A program may use at most 128 MiB of HBM per device.

v0:
```python
import math
import jax
import jax.numpy as jnp
from jax import lax
from jax.sharding import PartitionSpec as P


def extended(block, sides, width):
    for axis, dim in sides:
        count = lax.axis_size(axis)
        forward = [(i, i + 1) for i in range(count - 1)]
        backward = [(target, source) for source, target in forward]
        low = lax.ppermute(
            lax.slice_in_dim(block, block.shape[dim] - width, None, axis=dim), axis, forward
        )
        high = lax.ppermute(lax.slice_in_dim(block, 0, width, axis=dim), axis, backward)
        block = jnp.concatenate([low, block, high], axis=dim)
    return block


def conv_valid(kernel, field):
    result = lax.conv_general_dilated(
        field[None],
        kernel,
        (1, 1),
        "VALID",
        rhs_dilation=(8, 8),
        dimension_numbers=("NCHW", "HWOI", "NCHW"),
        preferred_element_type=jnp.float32,
    )
    return result[0]


def flipped(kernel):
    return jnp.transpose(kernel[::-1, ::-1], (0, 1, 3, 2))


def tap_grads(upper, field, base_r, base_c, rows, cols):
    taps = []
    for tap_r in range(3):
        line = []
        for tap_c in range(3):
            top = base_r + 8 * (tap_r - 1)
            left = base_c + 8 * (tap_c - 1)
            piece = field[:, top : top + rows, left : left + cols]
            line.append(
                lax.dot_general(
                    upper, piece, (((1, 2), (1, 2)), ((), ())), preferred_element_type=jnp.float32
                )
            )
        taps.append(jnp.stack(line))
    return jnp.stack(taps)


def slope(pre):
    sig = jax.nn.sigmoid(pre)
    return sig * (1.0 + pre * (1.0 - sig))


def inside_mask(row_first, col_first, margin, tile_rows, tile_cols, total_rows, total_cols):
    global_rows = row_first + jnp.arange(tile_rows + 2 * margin, dtype=jnp.int32) - margin
    global_cols = col_first + jnp.arange(tile_cols + 2 * margin, dtype=jnp.int32) - margin
    return ((global_rows >= 0) & (global_rows < total_rows))[:, None] & (
        (global_cols >= 0) & (global_cols < total_cols)
    )[None, :]


def shards(grad_out, row_feat, col_feat, conv_one, bias_one, conv_two):
    chans, tile_rows, tile_cols = grad_out.shape
    total_rows = tile_rows * lax.axis_size("row")
    total_cols = tile_cols * lax.axis_size("col")
    row_first = lax.axis_index("row") * tile_rows
    col_first = lax.axis_index("col") * tile_cols
    row_ext = extended(row_feat, (("row", 0),), 16)
    col_ext = extended(col_feat, (("col", 0),), 16)
    outer = inside_mask(row_first, col_first, 16, tile_rows, tile_cols, total_rows, total_cols)
    summed = row_ext.T.astype(jnp.float32)[:, :, None] + col_ext.T.astype(jnp.float32)[:, None, :]
    field = jnp.where(outer[None], summed, 0.0).astype(jnp.bfloat16)
    pre = conv_valid(conv_one, field) + bias_one[:, None, None]
    inside = inside_mask(row_first, col_first, 8, tile_rows, tile_cols, total_rows, total_cols)
    act = jnp.where(inside[None], jax.nn.silu(pre), 0.0).astype(jnp.bfloat16)
    grad_ext = extended(grad_out, (("row", 1), ("col", 2)), 16)
    back = conv_valid(flipped(conv_two), grad_ext)
    inner = jnp.where(inside[None], back * slope(pre), 0.0).astype(jnp.bfloat16)
    spread = conv_valid(flipped(conv_one), inner)
    inner_tile = inner[:, 8 : 8 + tile_rows, 8 : 8 + tile_cols]
    grad_in = grad_out.astype(jnp.float32) + spread
    row_part = jnp.sum(grad_in, axis=2).T
    col_part = jnp.sum(grad_in, axis=1).T
    grad_one = tap_grads(inner_tile, field, 16, 16, tile_rows, tile_cols)
    grad_two = tap_grads(grad_out, act, 8, 8, tile_rows, tile_cols)
    bias_part = jnp.sum(inner_tile.astype(jnp.float32), axis=(1, 2))
    row_grad = lax.psum(row_part, "col") / math.sqrt(total_cols)
    col_grad = lax.psum(col_part, "row") / math.sqrt(total_rows)
    sum_one, sum_bias, sum_two = lax.psum((grad_one, bias_part, grad_two), ("row", "col"))
    whole = math.sqrt(total_rows * total_cols)
    return (row_grad, col_grad, sum_one / whole, sum_bias / whole, sum_two / whole)


def solution(mesh):
    in_specs = (P(None, "row", "col"), P("row", None), P("col", None), P(), P(), P())
    out_specs = (P("row", None), P("col", None), P(), P(), P())
    return jax.shard_map(shards, mesh=mesh, in_specs=in_specs, out_specs=out_specs, check_vma=False)
```

profile of v0, /device:TPU:1, one launch (start us, length us, event | category | flops | bytes accessed | tf_op | source)
XLA Modules:
  0.0 769.2 jit_solution(11806747635135335982)
XLA Ops:
  7.2 4.2 collective-permute-start.4
  11.4 1.3 collective-permute-start.5
  12.7 0.8 fusion.84
  13.5 5.7 collective-permute-start.6
  19.3 1.9 collective-permute-start.7
  21.2 5.1 collective-permute-start
  26.5 3.6 copy.67
  30.4 1.3 collective-permute-start.1
  31.7 0.8 convert_bitcast_fusion
  32.7 0.7 convert_bitcast_fusion.1
  33.4 2.7 select_convert_fusion
  36.1 2.3 copy.77
  38.4 0.5 slice.100
  38.9 0.4 copy-done.12
  39.3 5.9 broadcast_select_fusion
  45.2 2.7 copy.84
  47.9 2.6 slice.105
  50.5 6.2 copy.124
  56.7 3.2 select_convert_fusion.2
  59.9 0.4 convolution_bitcast_fusion.3
  60.3 0.4 convolution_bitcast_fusion.4
  61.1 0.4 convolution_bitcast_fusion.6
  61.5 0.4 convolution_bitcast_fusion.7
  62.3 0.4 convolution_bitcast_fusion
  62.7 0.4 convolution_bitcast_fusion.1
  63.5 2.3 select_convert_fusion.1
  65.8 0.7 maximum_bitcast_fusion.3
  66.5 3.8 add_divide_fusion
  70.3 3.5 copy.69
  73.8 3.6 copy.71
  77.4 1.2 pad_maximum_fusion.5
  78.7 4.8 collective-permute-start.2
  83.5 1.9 collective-permute-start.3
  85.4 0.7 pad_maximum_fusion.2
  86.2 5.2 collective-permute-done.3
  91.4 5.1 pad_maximum_fusion
  96.5 2.3 copy.73
  98.8 0.5 slice.99
  99.4 6.2 multiply_multiply_fusion
  105.5 2.7 copy.82
  108.3 2.5 slice.104
  110.8 6.1 copy.123
  116.9 3.8 convert_reduce_fusion
  121.5 0.4 convolution_bitcast_fusion.14
  122.6 0.4 convolution_bitcast_fusion.15
  123.7 0.4 convolution_bitcast_fusion.9
  124.1 86.2 %psum.38 = f32[64]{0:T(128)S(1)} all-reduce(f32[64]{0:T(128)S(1)} %get-tuple-element.14), channel_id=1, replica_groups=mesh['row'=32,'col'=8] {'row','col'}, use_global_device_ids=true, to_apply=%region_6.7 | all-reduce | flops 64 | bytes 512 | tf_op jit(solution)/shard_map/psum | solution.py:95
  210.2 0.5 broadcast_multiply_fusion.4
  210.7 0.9 copy.78
  211.6 2.2 fusion.17
  213.9 1.4 copy.80
  215.7 2.0 fusion.33
  217.7 0.7 copy.81
  218.5 0.5 copy-done.3
  219.0 1.4 fusion.36
  220.4 14.5 %psum.35 = f32[16,64]{1,0:T(8,128)S(1)} all-reduce(f32[16,64]{1,0:T(8,128)S(1)} %bitcast.166), channel_id=1, replica_groups=mesh['row'=32,'col'=8] {'col'}, use_global_device_ids=true, to_apply=%region_1.2 | all-reduce | flops 1024 | bytes 8192 | tf_op jit(solution)/shard_map/psum | solution.py:93
  234.9 0.6 broadcast_multiply_fusion.3
  235.5 0.7 pad_maximum_fusion.1
  236.3 250.7 %all-reduce.4.cloned.1.call-done = f32[256,64]{1,0:T(8,128)} async-done(((f32[256,64]{1,0:T(8,128)}), f32[256,64]{1,0:T(8,128)}) %all-reduce.4.cloned.1.call-update) | async-done | bytes 65552 | tf_op jit(solution)/shard_map/psum | solution.py:94
  487.0 0.9 broadcast_multiply_fusion.2
  487.9 0.7 copy.104
  488.6 270.1 %all-reduce.6.cloned.1.call-done = (f32[3,3,64,64]{3,2,1,0:T(8,128)}, f32[3,3,64,64]{3,2,1,0:T(8,128)}) async-done(((f32[3,3,64,64]{3,2,1,0:T(8,128)}, f32[3,3,64,64]{3,2,1,0:T(8,128)}), (f32[3,3,64,64]{3,2,1,0:T(8,128)}, f32[3,3,64,64]{3,2,1,0:T(8,128)})) %all-reduce.6.cloned.1.call-update) | async-done | bytes 294928 | tf_op jit(solution)/shard_map/psum | solution.py:95
  758.7 1.7 broadcast_multiply_fusion
  760.4 1.7 broadcast_multiply_fusion.1
  (69 shorter events, 4.3 us)
Async XLA Ops:
  7.2 92.2 %copy-start = (bf16[3,3,64,64]{3,2,1,0:T(8,128)(2,1)S(1)}, bf16[3,3,64,64]{3,2,1,0:T(8,128)(2,1)}, u32[]{:S(2)}) copy-start(bf16[3,3,64,64]{3,2,1,0:T(8,128)(2,1)} %param.11) | copy-start | bytes 221188
  7.2 479.8 %all-reduce.4.cloned.1.call-start = ((), (), s32[]{:S(2)}) async-start(), calls=%async_computation | async-start | bytes 262144 | tf_op jit(solution)/shard_map/psum | solution.py:94
  7.2 25.5 %collective-permute-start.4 = (bf16[16,64]{1,0:T(8,128)(2,1)}, bf16[16,64]{1,0:T(8,128)(2,1)S(1)}, u32[]{:S(2)}, u32[]{:S(2)}) collective-permute-start(bf16[16,64]{1,0:T(8,128)(2,1)} %param.7), channel_id=1, source_target_pairs={{0,8},{8,16},{16,24},{24,32},{32,40},{40,48},{48,56},{56,64},{64,7... | collective-permute-start | bytes 6152 | tf_op jit(solution)/shard_map/ppermute | solution.py:13
  11.4 21.3 %collective-permute-start.5 = (bf16[16,64]{1,0:T(8,128)(2,1)}, bf16[16,64]{1,0:T(8,128)(2,1)S(1)}, u32[]{:S(2)}, u32[]{:S(2)}) collective-permute-start(bf16[16,64]{1,0:T(8,128)(2,1)} %param.7), channel_id=1, source_target_pairs={{8,0},{16,8},{24,16},{32,24},{40,32},{48,40},{56,48},{64,56},{72,6... | collective-permute-start | bytes 6152 | tf_op jit(solution)/shard_map/ppermute | solution.py:16
  13.5 16.9 %collective-permute-start.6 = (bf16[16,64]{0,1:T(8,128)(2,1)S(1)}, bf16[16,64]{0,1:T(8,128)(2,1)S(1)}, u32[]{:S(2)}, u32[]{:S(2)}) collective-permute-start(bf16[16,64]{0,1:T(8,128)(2,1)S(1)} %get-tuple-element.22), channel_id=1, source_target_pairs={{0,1},{1,2},{2,3},{3,4},{4,5},{5,6},{6,7},{8,9},{9,10},{10,11},{11... | collective-permute-start | bytes 6152 | tf_op jit(solution)/shard_map/ppermute | solution.py:13
  19.3 12.5 %collective-permute-start.7 = (bf16[16,64]{0,1:T(8,128)(2,1)S(1)}, bf16[16,64]{0,1:T(8,128)(2,1)S(1)}, u32[]{:S(2)}, u32[]{:S(2)}) collective-permute-start(bf16[16,64]{0,1:T(8,128)(2,1)S(1)} %get-tuple-element.23), channel_id=1, source_target_pairs={{1,0},{2,1},{3,2},{4,3},{5,4},{6,5},{7,6},{9,8},{10,9},{11,10},{12... | collective-permute-start | bytes 6152 | tf_op jit(solution)/shard_map/ppermute | solution.py:16
  21.2 49.1 %collective-permute-start = (bf16[64,16,256]{2,1,0:T(8,128)(2,1)}, bf16[64,16,256]{2,1,0:T(8,128)(2,1)}, u32[]{:S(2)}, u32[]{:S(2)}) collective-permute-start(bf16[64,16,256]{2,1,0:T(8,128)(2,1)} %param.6), channel_id=1, source_target_pairs={{0,8},{8,16},{16,24},{24,32},{32,40},{40,48},{48,56},{56,64},{64,7... | collective-permute-start | bytes 1572872 | tf_op jit(solution)/shard_map/ppermute | solution.py:13
  30.4 43.4 %collective-permute-start.1 = (bf16[64,16,256]{2,1,0:T(8,128)(2,1)}, bf16[64,16,256]{2,1,0:T(8,128)(2,1)}, u32[]{:S(2)}, u32[]{:S(2)}) collective-permute-start(bf16[64,16,256]{2,1,0:T(8,128)(2,1)} %param.6), channel_id=1, source_target_pairs={{8,0},{16,8},{24,16},{32,24},{40,32},{48,40},{56,48},{64,56},{72,6... | collective-permute-start | bytes 1572872 | tf_op jit(solution)/shard_map/ppermute | solution.py:16
  38.4 0.9 copy-start.12
  38.4 0.9 copy-start.15
  45.2 2.8 copy-start.6
  50.5 6.2 copy-start.11
  56.7 3.2 copy-start.9
  77.4 8.0 %copy-start.10 = (f32[1,3,64,64]{3,2,1,0:T(8,128)S(1)}, f32[1,3,64,64]{3,2,1,0:T(8,128)}, u32[]{:S(2)}) copy-start(f32[1,3,64,64]{3,2,1,0:T(8,128)} %get-tuple-element.29) | copy-start | bytes 147460
  77.4 14.0 %copy-start.2 = (bf16[64,16,256]{0,1,2:T(8,128)(2,1)S(1)}, bf16[64,16,256]{0,1,2:T(8,128)(2,1)}, u32[]{:S(2)}) copy-start(bf16[64,16,256]{0,1,2:T(8,128)(2,1)} %copy.67) | copy-start | bytes 1572868
  77.4 14.0 %copy-start.4 = (bf16[64,16,256]{0,1,2:T(8,128)(2,1)S(1)}, bf16[64,16,256]{0,1,2:T(8,128)(2,1)}, u32[]{:S(2)}) copy-start(bf16[64,16,256]{0,1,2:T(8,128)(2,1)} %copy.69) | copy-start | bytes 1572868
  77.4 14.0 %copy-start.5 = (bf16[64,16,256]{0,1,2:T(8,128)(2,1)S(1)}, bf16[64,16,256]{0,1,2:T(8,128)(2,1)}, u32[]{:S(2)}) copy-start(bf16[64,16,256]{0,1,2:T(8,128)(2,1)} %copy.71) | copy-start | bytes 1572868
  78.7 7.5 collective-permute-start.2
  83.5 7.9 %collective-permute-start.3 = (bf16[64,48,16]{0,1,2:T(8,128)(2,1)S(1)}, bf16[64,48,16]{0,1,2:T(8,128)(2,1)S(1)}, u32[]{:S(2)}, u32[]{:S(2)}) collective-permute-start(bf16[64,48,16]{0,1,2:T(8,128)(2,1)S(1)} %get-tuple-element.21), channel_id=1, source_target_pairs={{1,0},{2,1},{3,2},{4,3},{5,4},{6,5},{7,6},{9,8},{10,9},{11,10},{12... | collective-permute-start | bytes 294920 | tf_op jit(solution)/shard_map/ppermute | solution.py:16
  91.4 7.9 %slice-start = ((s8[4718592]{0:T(1024)(128)(4,1)}), s8[4194304]{0:T(1024)(128)(4,1)S(1)}, s32[]{:S(2)}) async-start(s8[4718592]{0:T(1024)(128)(4,1)} %bitcast.163), calls=%async_computation.2 | async-start | bytes 8388608
  96.5 2.8 slice-start.1
  116.9 3.8 copy-start.7
  121.8 88.9 %copy-start.8 = (bf16[32,8,36,64]{3,1,2,0:T(8,128)(2,1)S(1)}, bf16[32,8,36,64]{3,1,2,0:T(8,128)(2,1)}, u32[]{:S(2)}) copy-start(bf16[32,8,36,64]{3,1,2,0:T(8,128)(2,1)} %get-tuple-element.24) | copy-start | bytes 3538948
  213.9 1.8 copy-start.13
  213.9 1.8 copy-start.14
  217.7 1.2 copy-start.3
  218.5 543.7 %copy-start.1 = (bf16[3,3,64,64]{3,2,1,0:T(8,128)(2,1)S(1)}, bf16[3,3,64,64]{3,2,1,0:T(8,128)(2,1)}, u32[]{:S(2)}) copy-start(bf16[3,3,64,64]{3,2,1,0:T(8,128)(2,1)} %param.11) | copy-start | bytes 221188
  220.4 538.3 %all-reduce.6.cloned.1.call-start = ((), (), s32[]{:S(2)}) async-start(), calls=%async_computation.1 | async-start | bytes 1179648 | tf_op jit(solution)/shard_map/psum | solution.py:95
Sparse Core Ops, SparseCore 0:
  220.5 266.4 all-reduce.3
  494.1 264.5 all-reduce.5
where the time goes:
time: 772 us; the launch traced here: 769 us
  waiting for transfers between devices  526 us (68%)
  blocking collectives  101 us (13%)
  local copies, waits for them, and re-layouts  45.4 us (6%)
  other arithmetic  35.1 us (5%)
  starting transfers between devices  26.3 us (3%)
  matrix products  20.9 us (3%)
  between operations  14.8 us (2%)
    psum x1, waiting for transfers between devices, shards(): lax.psum((grad_one, bias_part, grad_two), ('row', 'col'))  270 us
    psum x1, waiting for transfers between devices, shards(): col_grad = lax.psum(col_part, 'row') / math.sqrt(total_rows)  251 us
    psum x1, blocking collectives, shards(): lax.psum((grad_one, bias_part, grad_two), ('row', 'col'))  86.2 us
    ppermute x4, starting transfers between devices, extended(): lax.ppermute(lax.slice_in_dim(block, block.shape[dim] - width, None, axis...  19.8 us
    conv_general_dilated x11, local copies, waits for them, and re-layouts, conv_valid(): lax.conv_general_dilated(field[None], kernel, (1, 1), 'VALID', rhs_dilati...  18.6 us
    unnamed x40, local copies, waits for them, and re-layouts  17.6 us
  transfers between devices with their start and end apart: 10, of which 3 were waited for; matrix products, arithmetic and copies ran while one was open for 7% of the time, Pallas kernels for 0%

commit v1 on v0

--- a/solution.py
+++ b/solution.py
@@ -92,7 +92,7 @@
     bias_part = jnp.sum(inner_tile.astype(jnp.float32), axis=(1, 2))
     row_grad = lax.psum(row_part, "col") / math.sqrt(total_cols)
     col_grad = lax.psum(col_part, "row") / math.sqrt(total_rows)
-    sum_one, sum_bias, sum_two = lax.psum((grad_one, bias_part, grad_two), ("row", "col"))
+    sum_one, sum_bias, sum_two = lax.psum(lax.psum((grad_one, bias_part, grad_two), "col"), "row")
     whole = math.sqrt(total_rows * total_cols)
     return (row_grad, col_grad, sum_one / whole, sum_bias / whole, sum_two / whole)
 

time: 772 us -> 562 us (0.73)
  the two profiles are of different devices: /device:TPU:1 before, /device:TPU:30 now
where the time goes in v1:
time: 562 us; the launch traced here: 559 us
  waiting for transfers between devices  316 us (56%)
  blocking collectives  101 us (18%)
  local copies, waits for them, and re-layouts  45.4 us (8%)
  other arithmetic  35.1 us (6%)
  starting transfers between devices  25.7 us (5%)
  matrix products  21.7 us (4%)
  between operations  14.9 us (3%)
    psum x1, waiting for transfers between devices, shards(): col_grad = lax.psum(col_part, 'row') / math.sqrt(total_rows)  312 us
    psum x1, blocking collectives, shards(): lax.psum(lax.psum((grad_one, bias_part, grad_two), 'col'), 'row')  78.1 us
    psum x1, blocking collectives, shards(): row_grad = lax.psum(row_part, 'col') / math.sqrt(total_cols)  22.9 us
    ppermute x4, starting transfers between devices, extended(): lax.ppermute(lax.slice_in_dim(block, block.shape[dim] - width, None, axis...  18.7 us
    conv_general_dilated x11, local copies, waits for them, and re-layouts, conv_valid(): lax.conv_general_dilated(field[None], kernel, (1, 1), 'VALID', rhs_dilati...  18.6 us
    unnamed x38, local copies, waits for them, and re-layouts  17.5 us
    conv_general_dilated x3, matrix products, conv_valid(): lax.conv_general_dilated(field[None], kernel, (1, 1), 'VALID', rhs_dilati...  14.9 us
  transfers between devices with their start and end apart: 10, of which 2 were waited for; matrix products, arithmetic and copies ran while one was open for 10% of the time, Pallas kernels for 0%

profile of v1, /device:TPU:30, one launch (start us, length us, event | category | flops | bytes accessed | tf_op | source)
XLA Modules:
  0.0 559.3 jit_solution(11250851058268903844)
XLA Ops:
  7.2 3.5 collective-permute-start.4
  10.8 2.4 collective-permute-start.5
  13.2 0.8 fusion.84
  14.0 1.3 collective-permute-start.6
  15.3 1.3 collective-permute-start.7
  16.6 7.6 %collective-permute-start = (bf16[64,16,256]{2,1,0:T(8,128)(2,1)}, bf16[64,16,256]{2,1,0:T(8,128)(2,1)}, u32[]{:S(2)}, u32[]{:S(2)}) collective-permute-start(bf16[64,16,256]{2,1,0:T(8,128)(2,1)} %param.6), channel_id=1, source_target_pairs={{0,8},{8,16},{16,24},{24,32},{32,40},{40,48},{48,56},{56,64},{64,7... | collective-permute-start | bytes 1572872 | tf_op jit(solution)/shard_map/ppermute | solution.py:13
  24.5 3.6 copy.67
  28.4 1.9 collective-permute-start.1
  30.3 0.8 convert_bitcast_fusion
  31.3 0.7 convert_bitcast_fusion.1
  32.0 2.7 select_convert_fusion
  34.7 2.3 copy.77
  37.0 0.5 slice.100
  37.5 0.4 copy-done.12
  37.9 5.9 %broadcast_select_fusion = f32[32,8,36,64]{3,1,2,0:T(8,128)S(1)} fusion(pred[8,36]{0,1:T(8,128)(4,1)S(1)} %copy-done.14, bf16[3,3,64,64]{3,2,1,0:T(8,128)(2,1)S(1)} %copy-done.12, bf16[64,48,1,7,16]{0,3,4,1,2:T(8,128)(2,1)S(1)} %slice.100, bf16[64,48,1,8,36]{0,3,4,1,2:T(8,128)(2,1)S(1)} %copy.77), kind=kOutput, calls=%fused_computation.34 | convolution fusion | flops 687734784 | bytes 4890912 | tf_op jit(solution)/shard_map/conv_general_dilated | solution.py:22
  43.8 2.7 copy.84
  46.6 2.6 slice.105
  49.1 6.1 %copy.124 = f32[32,1,272,64]{2,3,0,1:T(8,128)} copy(f32[32,1,272,64]{3,0,2,1:T(8,128)} %slice.105) | data formatting | bytes 4456448
  55.3 3.2 select_convert_fusion.2
  58.5 0.4 convolution_bitcast_fusion.3
  58.9 0.4 convolution_bitcast_fusion.4
  59.7 0.4 convolution_bitcast_fusion.6
  60.1 0.4 convolution_bitcast_fusion.7
  60.9 0.4 convolution_bitcast_fusion
  61.3 0.4 convolution_bitcast_fusion.1
  62.1 2.3 select_convert_fusion.1
  64.4 0.7 maximum_bitcast_fusion.3
  65.0 3.8 add_divide_fusion
  68.9 3.6 copy.69
  72.4 3.6 copy.71
  76.0 1.2 pad_maximum_fusion.5
  77.3 6.3 %collective-permute-start.2 = (bf16[64,48,16]{0,1,2:T(8,128)(2,1)S(1)}, bf16[64,48,16]{0,1,2:T(8,128)(2,1)S(1)}, u32[]{:S(2)}, u32[]{:S(2)}) collective-permute-start(bf16[64,48,16]{0,1,2:T(8,128)(2,1)S(1)} %get-tuple-element.25), channel_id=1, source_target_pairs={{0,1},{1,2},{2,3},{3,4},{4,5},{5,6},{6,7},{8,9},{9,10},{10,11},{11... | collective-permute-start | bytes 294920 | tf_op jit(solution)/shard_map/ppermute | solution.py:13
  83.5 1.3 collective-permute-start.3
  84.8 0.7 pad_maximum_fusion.2
  85.6 3.7 collective-permute-done.3
  89.3 5.1 pad_maximum_fusion
  94.4 2.3 copy.73
  96.7 0.5 slice.99
  97.2 6.2 %multiply_multiply_fusion = (bf16[32,8,36,64]{3,1,2,0:T(8,128)(2,1)}, f32[32,8,36,64]{3,1,2,0:T(8,128)S(1)}) fusion(f32[32,8,36,64]{3,1,2,0:T(8,128)S(1)} %bitcast.164, f32[64]{0:T(128)S(1)} %copy-done.11, bf16[3,3,64,64]{3,2,1,0:T(8,128)(2,1)S(1)} %copy-done, bf16[64,48,1,7,16]{0,3,4,1,2:T(8,128)(2,1)S(1)} %slice.99, ...), kind=kOutput, calls=%fused_computation.18 | convolution fusion | flops 693633024 | bytes 8430112 | tf_op jit(solution)/shard_map/conv_general_dilated | solution.py:22
  103.4 2.7 copy.82
  106.1 2.5 slice.104
  108.7 6.1 %copy.123 = f32[32,1,272,64]{2,3,0,1:T(8,128)} copy(f32[32,1,272,64]{3,0,2,1:T(8,128)} %slice.104) | data formatting | bytes 4456448
  114.8 3.8 convert_reduce_fusion
  118.6 0.4 convolution_bitcast_fusion.12
  119.0 0.4 convolution_bitcast_fusion.13
  120.4 0.4 convolution_bitcast_fusion.15
  121.6 0.4 convolution_bitcast_fusion.9
  121.9 0.9 copy.78
  122.9 2.2 fusion.17
  125.1 1.4 copy.80
  126.9 0.7 pad_maximum_fusion.1
  127.7 2.9 fusion.33
  130.7 0.7 copy.81
  131.4 0.5 copy-done.3
  131.9 1.4 fusion.36
  133.3 22.9 %all-reduce.1 = (f32[16,64]{1,0:T(8,128)S(1)}, f32[64]{0:T(128)S(1)}) all-reduce(f32[16,64]{1,0:T(8,128)S(1)} %bitcast.166, f32[64]{0:T(128)S(1)} %get-tuple-element.21), channel_id=1, replica_groups=mesh['row'=32,'col'=8] {'col'}, use_global_device_ids=true, to_apply=%region_1.2 | all-reduce | flops 1088 | bytes 8704 | tf_op jit(solution)/shard_map/psum | solution.py:93
  156.1 78.1 %psum.61 = f32[64]{0:T(128)S(1)} all-reduce(f32[64]{0:T(128)S(1)} %get-tuple-element.16), channel_id=1, replica_groups=mesh['row'=32,'col'=8] {'row'}, use_global_device_ids=true, to_apply=%region_8.9 | all-reduce | flops 64 | bytes 512 | tf_op jit(solution)/shard_map/psum | solution.py:95
  234.3 0.5 broadcast_multiply_fusion.4
  234.8 0.6 broadcast_multiply_fusion.3
  235.4 311.8 %all-reduce.6.cloned.1.call-done = (f32[256,64]{1,0:T(8,128)}, f32[3,3,64,64]{3,2,1,0:T(8,128)}, f32[3,3,64,64]{3,2,1,0:T(8,128)}) async-done(((f32[256,64]{1,0:T(8,128)}, f32[3,3,64,64]{3,2,1,0:T(8,128)}, f32[3,3,64,64]{3,2,1,0:T(8,128)}), (f32[256,64]{1,0:T(8,128)}, f32[3,3,64,64]{3,2,1,0:T(8,128)}, f32[3,3,64,64]{3,2,1,0:T(8,128)})) %all-reduce.6.cloned.1.call-update) | async-done | bytes 360464 | tf_op jit(solution)/shard_map/psum | solution.py:94
  547.2 1.7 broadcast_multiply_fusion
  548.9 1.7 broadcast_multiply_fusion.1
  550.6 0.9 broadcast_multiply_fusion.2
  551.5 0.7 copy.104
  (67 shorter events, 4.0 us)
Async XLA Ops:
  7.2 90.0 %copy-start = (bf16[3,3,64,64]{3,2,1,0:T(8,128)(2,1)S(1)}, bf16[3,3,64,64]{3,2,1,0:T(8,128)(2,1)}, u32[]{:S(2)}) copy-start(bf16[3,3,64,64]{3,2,1,0:T(8,128)(2,1)} %param.11) | copy-start | bytes 221188
  7.2 227.1 %all-reduce.8.cloned.1.call-start = ((), (), s32[]{:S(2)}) async-start(), calls=%async_computation.1 | async-start | bytes 1179648 | tf_op jit(solution)/shard_map/psum | solution.py:95
  7.2 24.1 %collective-permute-start.4 = (bf16[16,64]{1,0:T(8,128)(2,1)}, bf16[16,64]{1,0:T(8,128)(2,1)S(1)}, u32[]{:S(2)}, u32[]{:S(2)}) collective-permute-start(bf16[16,64]{1,0:T(8,128)(2,1)} %param.7), channel_id=1, source_target_pairs={{0,8},{8,16},{16,24},{24,32},{32,40},{40,48},{48,56},{56,64},{64,7... | collective-permute-start | bytes 6152 | tf_op jit(solution)/shard_map/ppermute | solution.py:13
  10.8 20.5 %collective-permute-start.5 = (bf16[16,64]{1,0:T(8,128)(2,1)}, bf16[16,64]{1,0:T(8,128)(2,1)S(1)}, u32[]{:S(2)}, u32[]{:S(2)}) collective-permute-start(bf16[16,64]{1,0:T(8,128)(2,1)} %param.7), channel_id=1, source_target_pairs={{8,0},{16,8},{24,16},{32,24},{40,32},{48,40},{56,48},{64,56},{72,6... | collective-permute-start | bytes 6152 | tf_op jit(solution)/shard_map/ppermute | solution.py:16
  14.0 14.4 %collective-permute-start.6 = (bf16[16,64]{0,1:T(8,128)(2,1)S(1)}, bf16[16,64]{0,1:T(8,128)(2,1)S(1)}, u32[]{:S(2)}, u32[]{:S(2)}) collective-permute-start(bf16[16,64]{0,1:T(8,128)(2,1)S(1)} %get-tuple-element.27), channel_id=1, source_target_pairs={{0,1},{1,2},{2,3},{3,4},{4,5},{5,6},{6,7},{8,9},{9,10},{10,11},{11... | collective-permute-start | bytes 6152 | tf_op jit(solution)/shard_map/ppermute | solution.py:13
  15.3 15.0 %collective-permute-start.7 = (bf16[16,64]{0,1:T(8,128)(2,1)S(1)}, bf16[16,64]{0,1:T(8,128)(2,1)S(1)}, u32[]{:S(2)}, u32[]{:S(2)}) collective-permute-start(bf16[16,64]{0,1:T(8,128)(2,1)S(1)} %get-tuple-element.28), channel_id=1, source_target_pairs={{1,0},{2,1},{3,2},{4,3},{5,4},{6,5},{7,6},{9,8},{10,9},{11,10},{12... | collective-permute-start | bytes 6152 | tf_op jit(solution)/shard_map/ppermute | solution.py:16
  16.6 52.2 %collective-permute-start = (bf16[64,16,256]{2,1,0:T(8,128)(2,1)}, bf16[64,16,256]{2,1,0:T(8,128)(2,1)}, u32[]{:S(2)}, u32[]{:S(2)}) collective-permute-start(bf16[64,16,256]{2,1,0:T(8,128)(2,1)} %param.6), channel_id=1, source_target_pairs={{0,8},{8,16},{16,24},{24,32},{32,40},{40,48},{48,56},{56,64},{64,7... | collective-permute-start | bytes 1572872 | tf_op jit(solution)/shard_map/ppermute | solution.py:13
  28.4 44.0 %collective-permute-start.1 = (bf16[64,16,256]{2,1,0:T(8,128)(2,1)}, bf16[64,16,256]{2,1,0:T(8,128)(2,1)}, u32[]{:S(2)}, u32[]{:S(2)}) collective-permute-start(bf16[64,16,256]{2,1,0:T(8,128)(2,1)} %param.6), channel_id=1, source_target_pairs={{8,0},{16,8},{24,16},{32,24},{40,32},{48,40},{56,48},{64,56},{72,6... | collective-permute-start | bytes 1572872 | tf_op jit(solution)/shard_map/ppermute | solution.py:16
  37.0 0.9 copy-start.12
  37.0 0.9 copy-start.14
  43.8 2.8 copy-start.6
  49.1 6.1 %copy-start.11 = (f32[64]{0:T(128)S(1)}, f32[64]{0:T(128)}, u32[]{:S(2)}) copy-start(f32[64]{0:T(128)} %param.10) | copy-start | bytes 772
  55.3 3.2 copy-start.9
  76.0 8.8 %copy-start.10 = (f32[1,3,64,64]{3,2,1,0:T(8,128)S(1)}, f32[1,3,64,64]{3,2,1,0:T(8,128)}, u32[]{:S(2)}) copy-start(f32[1,3,64,64]{3,2,1,0:T(8,128)} %get-tuple-element.34) | copy-start | bytes 147460
  76.0 13.3 %copy-start.2 = (bf16[64,16,256]{0,1,2:T(8,128)(2,1)S(1)}, bf16[64,16,256]{0,1,2:T(8,128)(2,1)}, u32[]{:S(2)}) copy-start(bf16[64,16,256]{0,1,2:T(8,128)(2,1)} %copy.67) | copy-start | bytes 1572868
  76.0 13.3 %copy-start.4 = (bf16[64,16,256]{0,1,2:T(8,128)(2,1)S(1)}, bf16[64,16,256]{0,1,2:T(8,128)(2,1)}, u32[]{:S(2)}) copy-start(bf16[64,16,256]{0,1,2:T(8,128)(2,1)} %copy.69) | copy-start | bytes 1572868
  76.0 13.3 %copy-start.5 = (bf16[64,16,256]{0,1,2:T(8,128)(2,1)S(1)}, bf16[64,16,256]{0,1,2:T(8,128)(2,1)}, u32[]{:S(2)}) copy-start(bf16[64,16,256]{0,1,2:T(8,128)(2,1)} %copy.71) | copy-start | bytes 1572868
  77.3 8.3 %collective-permute-start.2 = (bf16[64,48,16]{0,1,2:T(8,128)(2,1)S(1)}, bf16[64,48,16]{0,1,2:T(8,128)(2,1)S(1)}, u32[]{:S(2)}, u32[]{:S(2)}) collective-permute-start(bf16[64,48,16]{0,1,2:T(8,128)(2,1)S(1)} %get-tuple-element.25), channel_id=1, source_target_pairs={{0,1},{1,2},{2,3},{3,4},{4,5},{5,6},{6,7},{8,9},{9,10},{10,11},{11... | collective-permute-start | bytes 294920 | tf_op jit(solution)/shard_map/ppermute | solution.py:13
  83.5 5.7 %collective-permute-start.3 = (bf16[64,48,16]{0,1,2:T(8,128)(2,1)S(1)}, bf16[64,48,16]{0,1,2:T(8,128)(2,1)S(1)}, u32[]{:S(2)}, u32[]{:S(2)}) collective-permute-start(bf16[64,48,16]{0,1,2:T(8,128)(2,1)S(1)} %get-tuple-element.26), channel_id=1, source_target_pairs={{1,0},{2,1},{3,2},{4,3},{5,4},{6,5},{7,6},{9,8},{10,9},{11,10},{12... | collective-permute-start | bytes 294920 | tf_op jit(solution)/shard_map/ppermute | solution.py:16
  89.3 7.9 %slice-start = ((s8[4718592]{0:T(1024)(128)(4,1)}), s8[4194304]{0:T(1024)(128)(4,1)S(1)}, s32[]{:S(2)}) async-start(s8[4718592]{0:T(1024)(128)(4,1)} %bitcast.163), calls=%async_computation.2 | async-start | bytes 8388608
  94.4 2.8 slice-start.1
  114.8 3.8 copy-start.7
  119.7 2.2 copy-start.8
  125.1 2.6 copy-start.13
  127.7 419.5 %all-reduce.6.cloned.1.call-start = ((), (), s32[]{:S(2)}) async-start(), calls=%async_computation | async-start | bytes 1441792 | tf_op jit(solution)/shard_map/psum | solution.py:94
  130.6 1.2 copy-start.3
  130.6 421.6 %copy-start.1 = (bf16[3,3,64,64]{3,2,1,0:T(8,128)(2,1)S(1)}, bf16[3,3,64,64]{3,2,1,0:T(8,128)(2,1)}, u32[]{:S(2)}) copy-start(bf16[3,3,64,64]{3,2,1,0:T(8,128)(2,1)} %param.11) | copy-start | bytes 221188
Sparse Core Ops, SparseCore 0:
  127.8 81.8 all-reduce.7
  234.4 312.7 all-reduce.5
